TPU v7x, 32 devices: a whole 2x2x4 slice. The times are simulated.
32 devices in a mesh: room: 2 (over y), gx: 16 (over z, x, core).
Axes of the slice: x: 2, y: 2, z: 4, core: 2. Of those that a mesh axis runs over, the one named last changes fastest.
Arguments:
- pressure: float32 [256, 256, 256], P(('room', 'gx')), parts along dimension 0, may hold values from -6 to 6
- previous: float32 [256, 256, 256], P(('room', 'gx')), parts along dimension 0, may hold values from -6 to 6
- materials: int32 [256, 256, 256], P(('room', 'gx')), parts along dimension 0, may hold values from 0 to 15
- admittance: float32 [32], P('room'), parts along dimension 0, may hold values from 0.05 to 1
- absorption: float32 [32], P('room'), parts along dimension 0, may hold values from 0.01 to 0.3
- source_cell: int32 [2], P('room'), parts along dimension 0, may hold values from 0 to 8388607
- signal: float32 [8], P('room'), parts along dimension 0, may hold values from -6 to 6
- receivers: int32 [128], P('room'), parts along dimension 0, may hold values from 0 to 8388607, as said below
Outputs:
- pressure_out: float32 [256, 256, 256], P(('room', 'gx')), parts along dimension 0
- previous_out: float32 [256, 256, 256], P(('room', 'gx')), parts along dimension 0
- readings: float32 [8, 64], P('room'), parts along dimension 0
There are 2 independent parts, one for each index of `room`. A program takes and returns all parts, laid end to end along the dimension named above; each array names one. Nothing has to cross between parts.
Inputs may be any that keep to these rules, and one draw needn't show every extreme that they name: `receivers`: receiver r lies on a layer of the first dimension from (r mod (16)) * 8 to that plus 8 - 1.
All inputs are finite; a program needn't handle non-finite values.
Results may differ from a plain program's by a relative error of at most 0.00002.
Values sent between devices are 32-bit elements; how exact they have to be, the bound alone decides.
A program may use at most 64 MiB of HBM per device.

v0:
```python
import jax
import jax.numpy as jnp
from jax import lax
from jax.sharding import PartitionSpec as P

courant = 0.5773502691896258
courant_sq = 1.0 / 3.0


def extended_2(cells, sides, width):
    for axis, dim in sides:
        count = lax.axis_size(axis)
        ends = count - 1
        head = lax.slice_in_dim(cells, 0, width, axis=dim)
        tail = lax.slice_in_dim(cells, cells.shape[dim] - width, cells.shape[dim], axis=dim)
        cells = jnp.concatenate(
            [
                lax.ppermute(tail, axis, [(i, (i + 1) % count) for i in range(ends)]),
                cells,
                lax.ppermute(head, axis, [((i + 1) % count, i) for i in range(ends)]),
            ],
            axis=dim,
        )
    return cells


def outside_count(start_x, slab_width, grid_x, size_y, size_z):
    coord_x = start_x + jnp.arange(slab_width)
    coord_y = jnp.arange(size_y)
    coord_z = jnp.arange(size_z)
    edge_x = ((coord_x == 0) | (coord_x == grid_x - 1)).astype(jnp.float32)
    edge_y = ((coord_y == 0) | (coord_y == size_y - 1)).astype(jnp.float32)
    edge_z = ((coord_z == 0) | (coord_z == size_z - 1)).astype(jnp.float32)
    return edge_x[:, None, None] + edge_y[None, :, None] + edge_z[None, None, :]


def advance(extended, previous, loss_cell, inside, signal_value, source_x, source_y, source_z):
    padded = jnp.pad(extended, ((0, 0), (1, 1), (1, 1)))
    summed = padded[2:, 1:-1, 1:-1] + padded[:-2, 1:-1, 1:-1]
    summed = summed + padded[1:-1, 2:, 1:-1] + padded[1:-1, :-2, 1:-1]
    summed = summed + padded[1:-1, 1:-1, 2:] + padded[1:-1, 1:-1, :-2]
    current = extended[1:-1]
    following = (
        (2.0 - courant_sq * inside) * current + courant_sq * summed - (1.0 - loss_cell) * previous
    ) / (1.0 + loss_cell)
    slab_width = previous.shape[0]
    owner_mask = (source_x >= 0) & (source_x < slab_width)
    return following.at[jnp.clip(source_x, 0, slab_width - 1), source_y, source_z].add(
        jnp.where(owner_mask, signal_value, 0.0)
    )


def sample(field, receivers, start_x):
    plane_size = field.shape[1] * field.shape[2]
    local_x = receivers // plane_size - start_x
    offset = receivers % plane_size
    owner_mask = (local_x >= 0) & (local_x < field.shape[0])
    flat_index = jnp.clip(local_x, 0, field.shape[0] - 1) * plane_size + offset
    return jnp.where(owner_mask, field.reshape(-1)[flat_index], 0.0)


def collect(local_values):
    return lax.psum(local_values, "gx")


def local(pressure, previous, materials, admittance, absorption, source_cell, signal, receivers):
    slab_width, size_y, size_z = pressure.shape
    devices = lax.axis_size("gx")
    start_x = lax.axis_index("gx") * slab_width
    grid_x = slab_width * devices
    outside = outside_count(start_x, slab_width, grid_x, size_y, size_z)
    adm_cell = jnp.zeros(pressure.shape, jnp.float32)
    abs_cell = jnp.zeros(pressure.shape, jnp.float32)
    for material in range(admittance.shape[0]):
        chosen = materials == material
        adm_cell = jnp.where(chosen, admittance[material], adm_cell)
        abs_cell = jnp.where(chosen, absorption[material], abs_cell)
    loss_cell = 0.5 * courant * outside * adm_cell + abs_cell
    inside = 6.0 - outside
    source_flat = source_cell[0]
    source_x = source_flat // (size_y * size_z)
    source_y = source_flat // size_z % size_y
    source_z = source_flat % size_z
    samples = []
    for moment in range(signal.shape[0]):
        extended = extended_2(pressure, (("gx", 0),), 1)
        following = advance(
            extended,
            previous,
            loss_cell,
            inside,
            signal[moment],
            source_x - start_x,
            source_y,
            source_z,
        )
        samples.append(collect(sample(following, receivers, start_x)))
        previous, pressure = (pressure, following)
    readings = jnp.stack(samples)
    return (pressure, previous, readings)


def solution(mesh):
    placed = (
        P(("room", "gx"), None, None),
        P(("room", "gx"), None, None),
        P(("room", "gx"), None, None),
        P("room"),
        P("room"),
        P("room"),
        P("room"),
        P("room"),
    )
    return jax.shard_map(
        local,
        mesh=mesh,
        in_specs=placed,
        out_specs=(P(("room", "gx"), None, None), P(("room", "gx"), None, None), P("room", None)),
        check_vma=False,
    )
```

profile of v0, /device:TPU:0, one launch (start us, length us, event | category | flops | bytes accessed | tf_op | source)
XLA Modules:
  0.0 231.6 jit_solution(15854033556037329602)
XLA Ops:
  0.6 1.1 fusion.37
  1.7 2.4 %collective-permute-start.1 = (f32[1,256,256]{2,1,0:T(8,128)S(1)}, f32[1,256,256]{2,1,0:T(8,128)S(1)}, u32[]{:S(2)}, u32[]{:S(2)}) collective-permute-start(f32[1,256,256]{2,1,0:T(8,128)S(1)} %get-tuple-element.63), channel_id=1, source_target_pairs={{0,1},{1,2},{2,3},{3,4},{4,5},{5,6},{6,7},{7,8},{8,9},{9,10},{10,1... | collective-permute-start | bytes 786440 | tf_op jit(solution)/shard_map/ppermute | solution.py:18
  4.1 1.3 collective-permute-start
  6.1 1.5 fusion.38
  7.6 1.9 fusion.39
  9.5 2.0 fusion.40
  11.5 1.4 and_reduce_fusion
  13.6 0.1 broadcast_add_fusion
  13.7 0.0 collective-permute-done.1
  13.7 0.0 collective-permute-done
  13.7 3.6 %select_maximum_fusion.6 = f32[10,258,258]{2,1,0:T(8,128)S(1)} fusion(f32[1,256,256]{2,1,0:T(8,128)S(1)} %collective-permute-done, f32[8,256,256]{2,1,0:T(8,128)} %param.16, f32[1,256,256]{2,1,0:T(8,128)S(1)} %collective-permute-done.1), kind=kLoop, calls=%fused_computation.14 | loop fusion | flops 9984600 | bytes 5284000 | tf_op jit(solution)/shard_map/concatenate | solution.py:16
  17.3 26.0 %fusion.11 = f32[8,256,256]{2,1,0:T(8,128)S(1)} fusion(f32[8,256,256]{2,1,0:T(8,128)S(1)} %copy-done.9, f32[10,258,258]{2,1,0:T(8,128)S(1)} %select_maximum_fusion.6, f32[1,256,256]{2,1,0:T(8,128)S(1)} %collective-permute-done.1, f32[1,256,256]{2,1,0:T(8,128)S(1)} %collective-permute-done, f32[8,256,256]{2,1,0:T(8,128)S(1)} %copy-done.12, ...), kind=kLoop, calls=%fused_computation.29 | loop fusion | flops 36700160 | bytes 17310848 | tf_op jit(solution)/shard_map/div | solution.py:43
  43.3 0.6 dynamic-slice.33
  45.9 0.1 scatter-add.14
  46.1 5.1 %collective-permute-start.3 = (f32[1,256,256]{2,1,0:T(8,128)S(1)}, f32[1,256,256]{2,1,0:T(8,128)S(1)}, u32[]{:S(2)}, u32[]{:S(2)}) collective-permute-start(f32[1,256,256]{2,1,0:T(8,128)S(1)} %get-tuple-element.61), channel_id=1, source_target_pairs={{0,1},{1,2},{2,3},{3,4},{4,5},{5,6},{6,7},{7,8},{8,9},{9,10},{10,1... | collective-permute-start | bytes 786440 | tf_op jit(solution)/shard_map/ppermute | solution.py:18
  51.2 1.3 collective-permute-start.2
  53.2 0.0 copy-start.6
  53.2 0.0 copy-start.10
  53.2 0.0 collective-permute-done.3
  53.2 2.6 %collective-permute-done.2 = f32[1,256,256]{2,1,0:T(8,128)S(1)} collective-permute-done((f32[1,256,256]{2,1,0:T(8,128)S(1)}, f32[1,256,256]{2,1,0:T(8,128)S(1)}, u32[]{:S(2)}, u32[]{:S(2)}) %collective-permute-start.2) | collective-permute-done | bytes 262176 | tf_op jit(solution)/shard_map/ppermute | solution.py:20
  55.9 2.9 %select_maximum_fusion.4 = f32[10,258,258]{2,1,0:T(8,128)S(1)} fusion(f32[1,256,256]{2,1,0:T(8,128)S(1)} %collective-permute-done.2, f32[8,256,256]{2,1,0:T(8,128)S(1)} %scatter-add.14, f32[1,256,256]{2,1,0:T(8,128)S(1)} %collective-permute-done.3), kind=kLoop, calls=%fused_computation.12 | loop fusion | flops 9984600 | bytes 5284000 | tf_op jit(solution)/shard_map/concatenate | solution.py:16
  58.8 25.9 %fusion.14 = f32[8,256,256]{2,1,0:T(8,128)S(1)} fusion(f32[8,256,256]{2,1,0:T(8,128)S(1)} %scatter-add.14, f32[10,258,258]{2,1,0:T(8,128)S(1)} %select_maximum_fusion.4, f32[1,256,256]{2,1,0:T(8,128)S(1)} %collective-permute-done.3, f32[1,256,256]{2,1,0:T(8,128)S(1)} %collective-permute-done.2, f32[8,256,256]{2,1,0:T(8,128)S(1)} %copy-done.10, ...), kind=kLoop, calls=%fused_computation.32 | loop fusion | flops 36700160 | bytes 17310848 | tf_op jit(solution)/shard_map/div | solution.py:43
  84.7 0.0 copy-start
  84.7 1.3 copy-done
  86.0 0.6 dynamic-slice.34
  88.7 1.4 scatter-add.15
  90.1 1.1 fusion.35
  91.2 6.7 %collective-permute-start.5 = (f32[1,256,256]{2,1,0:T(8,128)S(1)}, f32[1,256,256]{2,1,0:T(8,128)S(1)}, u32[]{:S(2)}, u32[]{:S(2)}) collective-permute-start(f32[1,256,256]{2,1,0:T(8,128)S(1)} %get-tuple-element.59), channel_id=1, source_target_pairs={{0,1},{1,2},{2,3},{3,4},{4,5},{5,6},{6,7},{7,8},{8,9},{9,10},{10,1... | collective-permute-start | bytes 786440 | tf_op jit(solution)/shard_map/ppermute | solution.py:18
  97.8 1.3 collective-permute-start.4
  100.4 0.0 copy-start.1
  100.4 0.0 copy-start.7
  100.4 0.0 collective-permute-done.5
  100.4 0.9 collective-permute-done.4
  101.3 3.7 %select_maximum_fusion.2 = f32[10,258,258]{2,1,0:T(8,128)S(1)} fusion(f32[1,256,256]{2,1,0:T(8,128)S(1)} %collective-permute-done.4, f32[8,256,256]{2,1,0:T(8,128)} %scatter-add.15, f32[1,256,256]{2,1,0:T(8,128)S(1)} %collective-permute-done.5), kind=kLoop, calls=%fused_computation.10 | loop fusion | flops 9984600 | bytes 5284000 | tf_op jit(solution)/shard_map/concatenate | solution.py:16
  105.0 0.0 copy-done.1
  105.0 0.0 copy-done.7
  105.0 0.0 copy-start.13
  105.1 26.0 %fusion.17 = f32[8,256,256]{2,1,0:T(8,128)S(1)} fusion(f32[8,256,256]{2,1,0:T(8,128)S(1)} %copy-done.1, f32[10,258,258]{2,1,0:T(8,128)S(1)} %select_maximum_fusion.2, f32[1,256,256]{2,1,0:T(8,128)S(1)} %collective-permute-done.5, f32[1,256,256]{2,1,0:T(8,128)S(1)} %collective-permute-done.4, f32[8,256,256]{2,1,0:T(8,128)S(1)} %scatter-add.14, ...), kind=kLoop, calls=%fused_computation.35 | loop fusion | flops 36700160 | bytes 17310848 | tf_op jit(solution)/shard_map/div | solution.py:43
  131.0 0.0 copy-start.3
  131.0 1.3 copy-done.3
  132.4 0.6 dynamic-slice.35
  134.8 1.4 scatter-add.16
  136.1 1.1 fusion.34
  137.2 7.5 %collective-permute-start.7 = (f32[1,256,256]{2,1,0:T(8,128)S(1)}, f32[1,256,256]{2,1,0:T(8,128)S(1)}, u32[]{:S(2)}, u32[]{:S(2)}) collective-permute-start(f32[1,256,256]{2,1,0:T(8,128)S(1)} %get-tuple-element.57), channel_id=1, source_target_pairs={{0,1},{1,2},{2,3},{3,4},{4,5},{5,6},{6,7},{7,8},{8,9},{9,10},{10,1... | collective-permute-start | bytes 786440 | tf_op jit(solution)/shard_map/ppermute | solution.py:18
  144.8 1.5 collective-permute-start.6
  146.3 2.4 %copy.11 = f32[256,2,8,128]{3,1,2,0:T(2,128)} copy(f32[256,2,8,128]{3,2,1,0:T(8,128)S(1)} %bitcast.65) | data formatting | bytes 4194304
  148.7 1.7 gather_fusion
  150.4 4.1 %copy.12 = f32[256,2,8,128]{3,1,2,0:T(2,128)} copy(f32[256,2,8,128]{3,2,1,0:T(8,128)} %bitcast.66) | data formatting | bytes 4194304
  154.5 1.7 gather_fusion.1
  156.2 2.4 %copy.13 = f32[256,2,8,128]{3,1,2,0:T(2,128)} copy(f32[256,2,8,128]{3,2,1,0:T(8,128)S(1)} %bitcast.67) | data formatting | bytes 4194304
  158.6 1.7 gather_fusion.2
  160.3 0.0 copy-start.8
  160.3 0.0 collective-permute-done.7
  160.3 0.0 collective-permute-done.6
  160.4 2.9 %select_maximum_fusion = f32[10,258,258]{2,1,0:T(8,128)S(1)} fusion(f32[1,256,256]{2,1,0:T(8,128)S(1)} %collective-permute-done.6, f32[8,256,256]{2,1,0:T(8,128)S(1)} %copy-done.4, f32[1,256,256]{2,1,0:T(8,128)S(1)} %collective-permute-done.7), kind=kLoop, calls=%fused_computation.8 | loop fusion | flops 9984600 | bytes 5284000 | tf_op jit(solution)/shard_map/concatenate | solution.py:16
  163.3 25.9 %fusion.20 = f32[8,256,256]{2,1,0:T(8,128)S(1)} fusion(f32[8,256,256]{2,1,0:T(8,128)S(1)} %copy-done.4, f32[10,258,258]{2,1,0:T(8,128)S(1)} %select_maximum_fusion, f32[1,256,256]{2,1,0:T(8,128)S(1)} %collective-permute-done.7, f32[1,256,256]{2,1,0:T(8,128)S(1)} %collective-permute-done.6, f32[8,256,256]{2,1,0:T(8,128)S(1)} %copy-done.2, ...), kind=kLoop, calls=%fused_computation.38 | loop fusion | flops 36700160 | bytes 17310848 | tf_op jit(solution)/shard_map/div | solution.py:43
  189.2 0.0 copy-start.11
  189.2 1.3 copy-done.11
  190.5 0.6 dynamic-slice.36
  193.1 1.4 scatter-add.19
  194.5 2.7 %copy.14 = f32[256,2,8,128]{3,1,2,0:T(2,128)S(1)} copy(f32[256,2,8,128]{3,2,1,0:T(8,128)} %bitcast.68) | data formatting | bytes 4194304
  197.1 0.8 gather_fusion.3
  197.9 33.1 %all-reduce.4 = (f32[1,64]{1,0:T(1,128)S(1)}, f32[1,64]{1,0:T(1,128)S(1)}, f32[1,64]{1,0:T(1,128)S(1)}, f32[1,64]{1,0:T(1,128)S(1)}) all-reduce(f32[1,64]{1,0:T(1,128)S(1)} %get-tuple-element.67, f32[1,64]{1,0:T(1,128)S(1)} %get-tuple-element.66, f32[1,64]{1,0:T(1,128)S(1)} %get-tuple-element.68, ...), channel_id=1, replica_groups=mesh['room'=2,'gx'=16] {'gx'}, use_global_device_ids=true, to_apply=%region_4.5 | all-reduce | flops 256 | bytes 2048 | tf_op jit(solution)/shard_map/psum | solution.py:63
  231.0 0.6 pad_maximum_fusion.8
  (20 shorter events, 0.1 us)
Async XLA Ops:
  1.7 12.0 %collective-permute-start.1 = (f32[1,256,256]{2,1,0:T(8,128)S(1)}, f32[1,256,256]{2,1,0:T(8,128)S(1)}, u32[]{:S(2)}, u32[]{:S(2)}) collective-permute-start(f32[1,256,256]{2,1,0:T(8,128)S(1)} %get-tuple-element.63), channel_id=1, source_target_pairs={{0,1},{1,2},{2,3},{3,4},{4,5},{5,6},{6,7},{7,8},{8,9},{9,10},{10,1... | collective-permute-start | bytes 786440 | tf_op jit(solution)/shard_map/ppermute | solution.py:18
  4.1 9.6 %collective-permute-start = (f32[1,256,256]{2,1,0:T(8,128)S(1)}, f32[1,256,256]{2,1,0:T(8,128)S(1)}, u32[]{:S(2)}, u32[]{:S(2)}) collective-permute-start(f32[1,256,256]{2,1,0:T(8,128)S(1)} %get-tuple-element.64), channel_id=1, source_target_pairs={{1,0},{2,1},{3,2},{4,3},{5,4},{6,5},{7,6},{8,7},{9,8},{10,9},{11,1... | collective-permute-start | bytes 786440 | tf_op jit(solution)/shard_map/ppermute | solution.py:20
  13.7 3.6 %copy-start.5 = (s32[8,256,256]{2,1,0:T(8,128)S(1)}, s32[8,256,256]{2,1,0:T(8,128)}, u32[]{:S(2)}) copy-start(s32[8,256,256]{2,1,0:T(8,128)} %param.18) | copy-start | bytes 6291460
  13.7 3.6 %copy-start.9 = (f32[8,256,256]{2,1,0:T(8,128)S(1)}, f32[8,256,256]{2,1,0:T(8,128)}, u32[]{:S(2)}) copy-start(f32[8,256,256]{2,1,0:T(8,128)} %param.16) | copy-start | bytes 6291460
  13.7 3.6 %copy-start.12 = (f32[8,256,256]{2,1,0:T(8,128)S(1)}, f32[8,256,256]{2,1,0:T(8,128)}, u32[]{:S(2)}) copy-start(f32[8,256,256]{2,1,0:T(8,128)} %param.17) | copy-start | bytes 6291460
  46.1 7.1 %collective-permute-start.3 = (f32[1,256,256]{2,1,0:T(8,128)S(1)}, f32[1,256,256]{2,1,0:T(8,128)S(1)}, u32[]{:S(2)}, u32[]{:S(2)}) collective-permute-start(f32[1,256,256]{2,1,0:T(8,128)S(1)} %get-tuple-element.61), channel_id=1, source_target_pairs={{0,1},{1,2},{2,3},{3,4},{4,5},{5,6},{6,7},{7,8},{8,9},{9,10},{10,1... | collective-permute-start | bytes 786440 | tf_op jit(solution)/shard_map/ppermute | solution.py:18
  51.2 4.7 %collective-permute-start.2 = (f32[1,256,256]{2,1,0:T(8,128)S(1)}, f32[1,256,256]{2,1,0:T(8,128)S(1)}, u32[]{:S(2)}, u32[]{:S(2)}) collective-permute-start(f32[1,256,256]{2,1,0:T(8,128)S(1)} %get-tuple-element.62), channel_id=1, source_target_pairs={{1,0},{2,1},{3,2},{4,3},{5,4},{6,5},{7,6},{8,7},{9,8},{10,9},{11,1... | collective-permute-start | bytes 786440 | tf_op jit(solution)/shard_map/ppermute | solution.py:20
  53.2 5.6 %copy-start.6 = (s32[8,256,256]{2,1,0:T(8,128)S(1)}, s32[8,256,256]{2,1,0:T(8,128)}, u32[]{:S(2)}) copy-start(s32[8,256,256]{2,1,0:T(8,128)} %param.18) | copy-start | bytes 6291460
  53.2 5.6 %copy-start.10 = (f32[8,256,256]{2,1,0:T(8,128)S(1)}, f32[8,256,256]{2,1,0:T(8,128)}, u32[]{:S(2)}) copy-start(f32[8,256,256]{2,1,0:T(8,128)} %param.16) | copy-start | bytes 6291460
  84.7 1.3 copy-start
  91.2 9.2 %collective-permute-start.5 = (f32[1,256,256]{2,1,0:T(8,128)S(1)}, f32[1,256,256]{2,1,0:T(8,128)S(1)}, u32[]{:S(2)}, u32[]{:S(2)}) collective-permute-start(f32[1,256,256]{2,1,0:T(8,128)S(1)} %get-tuple-element.59), channel_id=1, source_target_pairs={{0,1},{1,2},{2,3},{3,4},{4,5},{5,6},{6,7},{7,8},{8,9},{9,10},{10,1... | collective-permute-start | bytes 786440 | tf_op jit(solution)/shard_map/ppermute | solution.py:18
  97.8 3.4 %collective-permute-start.4 = (f32[1,256,256]{2,1,0:T(8,128)S(1)}, f32[1,256,256]{2,1,0:T(8,128)S(1)}, u32[]{:S(2)}, u32[]{:S(2)}) collective-permute-start(f32[1,256,256]{2,1,0:T(8,128)S(1)} %get-tuple-element.60), channel_id=1, source_target_pairs={{1,0},{2,1},{3,2},{4,3},{5,4},{6,5},{7,6},{8,7},{9,8},{10,9},{11,1... | collective-permute-start | bytes 786440 | tf_op jit(solution)/shard_map/ppermute | solution.py:20
  100.4 4.7 %copy-start.1 = (f32[8,256,256]{2,1,0:T(8,128)S(1)}, f32[8,256,256]{2,1,0:T(8,128)}, u32[]{:S(2)}) copy-start(f32[8,256,256]{2,1,0:T(8,128)} %scatter-add.15) | copy-start | bytes 6291460
  100.4 4.7 %copy-start.7 = (s32[8,256,256]{2,1,0:T(8,128)S(1)}, s32[8,256,256]{2,1,0:T(8,128)}, u32[]{:S(2)}) copy-start(s32[8,256,256]{2,1,0:T(8,128)} %param.18) | copy-start | bytes 6291460
  105.0 41.2 %copy-start.13 = (s32[64]{0:T(128)S(1)}, s32[64]{0:T(128)}, u32[]{:S(2)}) copy-start(s32[64]{0:T(128)} %param.23) | copy-start | bytes 772
  131.0 1.3 copy-start.3
  137.2 23.1 %collective-permute-start.7 = (f32[1,256,256]{2,1,0:T(8,128)S(1)}, f32[1,256,256]{2,1,0:T(8,128)S(1)}, u32[]{:S(2)}, u32[]{:S(2)}) collective-permute-start(f32[1,256,256]{2,1,0:T(8,128)S(1)} %get-tuple-element.57), channel_id=1, source_target_pairs={{0,1},{1,2},{2,3},{3,4},{4,5},{5,6},{6,7},{7,8},{8,9},{9,10},{10,1... | collective-permute-start | bytes 786440 | tf_op jit(solution)/shard_map/ppermute | solution.py:18
  144.8 15.6 %collective-permute-start.6 = (f32[1,256,256]{2,1,0:T(8,128)S(1)}, f32[1,256,256]{2,1,0:T(8,128)S(1)}, u32[]{:S(2)}, u32[]{:S(2)}) collective-permute-start(f32[1,256,256]{2,1,0:T(8,128)S(1)} %get-tuple-element.58), channel_id=1, source_target_pairs={{1,0},{2,1},{3,2},{4,3},{5,4},{6,5},{7,6},{8,7},{9,8},{10,9},{11,1... | collective-permute-start | bytes 786440 | tf_op jit(solution)/shard_map/ppermute | solution.py:20
  150.4 5.8 %copy-start.4 = (f32[8,256,256]{2,1,0:T(8,128)S(1)}, f32[8,256,256]{2,1,0:T(8,128)}, u32[]{:S(2)}) copy-start(f32[8,256,256]{2,1,0:T(8,128)} %scatter-add.16) | copy-start | bytes 6291460
  160.3 3.0 %copy-start.2 = (f32[8,256,256]{2,1,0:T(8,128)S(1)}, f32[8,256,256]{2,1,0:T(8,128)}, u32[]{:S(2)}) copy-start(f32[8,256,256]{2,1,0:T(8,128)} %scatter-add.15) | copy-start | bytes 6291460
  160.3 3.0 %copy-start.8 = (s32[8,256,256]{2,1,0:T(8,128)S(1)}, s32[8,256,256]{2,1,0:T(8,128)}, u32[]{:S(2)}) copy-start(s32[8,256,256]{2,1,0:T(8,128)} %param.18) | copy-start | bytes 6291460
  189.2 1.3 copy-start.11
where the time goes:
time: 234 us; the launch traced here: 232 us
  other arithmetic  119 us (51%)
  local copies, waits for them, and re-layouts  36.7 us (16%)
  blocking collectives  33.1 us (14%)
  starting transfers between devices  27.1 us (12%)
  between operations  12.1 us (5%)
  waiting for transfers between devices  3.54 us (2%)
    div x4, other arithmetic, advance(): ((2.0 - courant_sq * inside) * current + courant_sq * summed - (1.0 - los...  104 us
    psum x1, blocking collectives, collect(): return lax.psum(local_values, 'gx')  33.1 us
    ppermute x4, starting transfers between devices, extended_2(): lax.ppermute(tail, axis, [(i, (i + 1) % count) for i in range(ends)])  21.7 us
    unnamed x32, local copies, waits for them, and re-layouts  15.6 us
    concatenate x4, other arithmetic, extended_2(): jnp.concatenate([lax.ppermute(tail, axis, [(i, (i + 1) % count) for i in...  13.1 us
    gather x4, local copies, waits for them, and re-layouts, sample(): return jnp.where(owner_mask, field.reshape(-1)[flat_index], 0.0)  5.82 us
    ppermute x4, starting transfers between devices, extended_2(): lax.ppermute(head, axis, [((i + 1) % count, i) for i in range(ends)])  5.35 us
  transfers between devices with their start and end apart: 8, of which 2 were waited for; matrix products, arithmetic and copies ran while one was open for 9% of the time, Pallas kernels for 0%

commit v1 on v0

v1 whole, which is shorter than its diff:
```python
import functools

import jax
import jax.numpy as jnp
from jax import lax
from jax.experimental import pallas as pl
from jax.experimental.pallas import tpu as pltpu
from jax.sharding import PartitionSpec as P

courant = 0.5773502691896258
courant_sq = 1.0 / 3.0

STRIPS = 4


def kernel(
    groups,
    steps,
    adm_ref,
    abs_ref,
    source_ref,
    signal_ref,
    recv_ref,
    pressure_ref,
    previous_ref,
    materials_ref,
    field,
    readings_ref,
    mats,
    coef,
    halo,
    mine,
    gathered,
    load_sem,
    first_send,
    send_sem,
    halo_sem,
    gather_send,
    gather_recv,
):
    layers, size_y, size_z = pressure_ref.shape
    rows = size_y // STRIPS
    receivers = recv_ref.shape[0]
    classes = adm_ref.shape[0]
    me = lax.axis_index("gx")
    start_x = me * layers
    has_left = me > 0
    has_right = me < groups - 1

    loads = [
        pltpu.make_async_copy(materials_ref, mats, load_sem.at[0]),
        pltpu.make_async_copy(pressure_ref, field.at[0], load_sem.at[1]),
        pltpu.make_async_copy(previous_ref, field.at[1], load_sem.at[2]),
    ]
    for load in loads:
        load.start()

    barrier = pltpu.get_barrier_semaphore()

    def greet(hop, carry):
        pl.semaphore_signal(barrier, inc=1, device_id={"gx": lax.rem(me + hop, groups)}, device_id_type=pl.DeviceIdType.MESH)
        return carry

    lax.fori_loop(1, groups, greet, 0)
    pl.semaphore_wait(barrier, groups - 1)

    def first_copy(side, strip):
        layer = layers - 1 if side == 0 else 0
        return pltpu.make_async_remote_copy(
            src_ref=pressure_ref.at[layer, pl.ds(strip * rows, rows), :],
            dst_ref=halo.at[0, side, strip],
            send_sem=first_send.at[side, strip],
            recv_sem=halo_sem.at[0, side, strip],
            device_id={"gx": me + 1 if side == 0 else me - 1},
            device_id_type=pl.DeviceIdType.MESH,
        )

    def step_copy(step, side, strip):
        layer = layers - 1 if side == 0 else 0
        return pltpu.make_async_remote_copy(
            src_ref=field.at[lax.rem(step + 1, 2), layer, pl.ds(pl.multiple_of(strip * rows, rows), rows), :],
            dst_ref=halo.at[step + 1, side, strip],
            send_sem=send_sem.at[step, side, strip],
            recv_sem=halo_sem.at[step + 1, side, strip],
            device_id={"gx": me + 1 if side == 0 else me - 1},
            device_id_type=pl.DeviceIdType.MESH,
        )

    for strip in range(STRIPS):
        pl.when(has_right)(lambda: first_copy(0, strip).start())
        pl.when(has_left)(lambda: first_copy(1, strip).start())

    lane = lax.broadcasted_iota(jnp.int32, (8, 128), 1)
    outside_lane = lane // classes
    class_lane = lane - outside_lane * classes
    adm_lane = jnp.zeros((8, 128), jnp.float32)
    abs_lane = jnp.zeros((8, 128), jnp.float32)
    for m in range(classes):
        adm_lane = jnp.where(class_lane == m, adm_ref[m], adm_lane)
        abs_lane = jnp.where(class_lane == m, abs_ref[m], abs_lane)
    table = courant_sq / (1.0 + (0.5 * courant * outside_lane.astype(jnp.float32) * adm_lane + abs_lane))

    loads[0].wait()
    block = 64
    table_block = jnp.broadcast_to(table[0:1], (block, 128))

    def fill(i, carry):
        layer = i // (size_y // block)
        row0 = pl.multiple_of(lax.rem(i, size_y // block) * block, block)
        at_x = start_x + layer
        edge_x = jnp.where((at_x == 0) | (at_x == groups * layers - 1), classes, 0)
        row = row0 + lax.broadcasted_iota(jnp.int32, (block, 128), 0)
        edge_xy = edge_x + jnp.where((row == 0) | (row == size_y - 1), classes, 0)
        for part in range(size_z // 128):
            cols = pl.ds(part * 128, 128)
            index = mats[layer, pl.ds(row0, block), cols] + edge_xy
            col = part * 128 + lax.broadcasted_iota(jnp.int32, (block, 128), 1)
            index = index + jnp.where((col == 0) | (col == size_z - 1), classes, 0)
            coef[layer, pl.ds(row0, block), cols] = jnp.take_along_axis(table_block, index, axis=1, mode="promise_in_bounds")
        return carry

    lax.fori_loop(0, layers * (size_y // block), fill, 0)
    loads[1].wait()
    loads[2].wait()

    source = source_ref[0]
    source_x = source // (size_y * size_z) - start_x
    source_y = (source // size_z) % size_y
    source_z = source % size_z

    row_id = lax.broadcasted_iota(jnp.int32, (rows, size_z), 0)
    col_id = lax.broadcasted_iota(jnp.int32, (rows, size_z), 1)
    mine[...] = jnp.zeros(mine.shape, jnp.float32)
    wide = mine.shape[1]
    mine_row = lax.broadcasted_iota(jnp.int32, mine.shape, 0)
    mine_col = lax.broadcasted_iota(jnp.int32, mine.shape, 1)
    lane_row = lax.broadcasted_iota(jnp.int32, (1, size_z), 1)

    def one_layer(step, now, then, strip, layer, low, high):
        row0 = pl.multiple_of(strip * rows, rows)
        here = pl.ds(row0, rows)
        c = field[now, layer, here, :]
        above = field[now, layer, pl.ds(jnp.maximum(row0 - 1, 0), 1), :]
        below = field[now, layer, pl.ds(jnp.minimum(row0 + rows, size_y - 1), 1), :]
        total = low + high
        total = total + jnp.where(row_id == 0, above, pltpu.roll(c, 1, 0))
        total = total + jnp.where(row_id == rows - 1, below, pltpu.roll(c, rows - 1, 0))
        total = total + jnp.where(col_id == 0, c, pltpu.roll(c, 1, 1))
        total = total + jnp.where(col_id == size_z - 1, c, pltpu.roll(c, size_z - 1, 1))
        old = field[then, layer, here, :]
        following = old + coef[layer, here, :] * (total - 6.0 * old)
        push = jnp.where(source_x == layer, signal_ref[step], 0.0)
        push = jnp.where(lane_row == source_z, push, 0.0)
        following = following + jnp.where(row_id == source_y - row0, push, 0.0)
        field[then, layer, here, :] = following

    def strip_body(step, strip):
        now = lax.rem(step, 2)
        then = 1 - now
        here = pl.ds(pl.multiple_of(strip * rows, rows), rows)

        @pl.when(has_left)
        def _():
            pltpu.make_async_copy(halo.at[step, 0, strip], halo.at[step, 0, strip], halo_sem.at[step, 0, strip]).wait()

        @pl.when(has_right)
        def _():
            pltpu.make_async_copy(halo.at[step, 1, strip], halo.at[step, 1, strip], halo_sem.at[step, 1, strip]).wait()

        pl.when((step >= 2) & has_right)(lambda: step_copy(step - 2, 0, strip).wait_send())
        pl.when((step >= 2) & has_left)(lambda: step_copy(step - 2, 1, strip).wait_send())

        first = field[now, 0, here, :]
        last = field[now, layers - 1, here, :]
        low = jnp.where(has_left, halo[step, 0, strip], first)
        high = jnp.where(has_right, halo[step, 1, strip], last)
        one_layer(step, now, then, strip, 0, low, field[now, 1, here, :])
        one_layer(step, now, then, strip, layers - 1, field[now, layers - 2, here, :], high)

        pl.when((step < steps - 1) & has_right)(lambda: step_copy(step, 0, strip).start())
        pl.when((step < steps - 1) & has_left)(lambda: step_copy(step, 1, strip).start())

        for layer in range(1, layers - 1):
            one_layer(step, now, then, strip, layer, field[now, layer - 1, here, :], field[now, layer + 1, here, :])

    def step_body(step, carry):
        def inner(strip, c):
            strip_body(step, strip)
            return c

        lax.fori_loop(0, STRIPS, inner, 0)
        then = lax.rem(step + 1, 2)
        total = mine[...]
        for k in range(receivers // groups):
            slot = k * groups + me
            cell = recv_ref[slot]
            at_x = jnp.clip(cell // (size_y * size_z) - start_x, 0, layers - 1)
            at_y = (cell // size_z) % size_y
            at_z = cell % size_z
            line = field[then, at_x, pl.ds(at_y, 1), :]
            value = jnp.sum(jnp.where(lane_row == at_z, line, 0.0), axis=1, keepdims=True)
            total = total + jnp.where((mine_row == step) & (mine_col == slot), value, 0.0)
        mine[...] = total
        return carry

    lax.fori_loop(0, steps, step_body, 0)

    def gather_copy(hop):
        peer = lax.rem(me + hop, groups)
        return pltpu.make_async_remote_copy(
            src_ref=mine,
            dst_ref=gathered.at[hop],
            send_sem=gather_send.at[hop],
            recv_sem=gather_recv.at[hop],
            device_id={"gx": peer},
            device_id_type=pl.DeviceIdType.MESH,
        )

    def gather_start(hop, carry):
        gather_copy(hop).start()
        return carry

    lax.fori_loop(1, groups, gather_start, 0)

    for strip in range(STRIPS):
        pl.when(has_right)(lambda: first_copy(0, strip).wait_send())
        pl.when(has_left)(lambda: first_copy(1, strip).wait_send())
        pl.when(has_right)(lambda: step_copy(steps - 2, 0, strip).wait_send())
        pl.when(has_left)(lambda: step_copy(steps - 2, 1, strip).wait_send())

    def gather_add(hop, total):
        gather_copy(hop).wait()
        return total + gathered[hop]

    total = lax.fori_loop(1, groups, gather_add, mine[...])
    readings_ref[...] = total[0:steps, 0:receivers]


def local(pressure, previous, materials, admittance, absorption, source_cell, signal, receivers):
    layers, size_y, size_z = pressure.shape
    groups = lax.axis_size("gx")
    steps = signal.shape[0]
    wide = -(-receivers.shape[0] // 128) * 128
    rows = size_y // STRIPS
    smem = pl.BlockSpec(memory_space=pltpu.SMEM)
    vmem = pl.BlockSpec(memory_space=pltpu.VMEM)
    hbm = pl.BlockSpec(memory_space=pl.ANY)
    field, readings = pl.pallas_call(
        functools.partial(kernel, groups, steps),
        out_shape=(
            jax.ShapeDtypeStruct((2, layers, size_y, size_z), jnp.float32),
            jax.ShapeDtypeStruct((steps, receivers.shape[0]), jnp.float32),
        ),
        in_specs=[smem] * 5 + [hbm] * 3,
        out_specs=(vmem, vmem),
        scratch_shapes=[
            pltpu.VMEM((layers, size_y, size_z), jnp.int32),
            pltpu.VMEM((layers, size_y, size_z), jnp.float32),
            pltpu.VMEM((steps, 2, STRIPS, rows, size_z), jnp.float32),
            pltpu.VMEM((8, wide), jnp.float32),
            pltpu.VMEM((groups, 8, wide), jnp.float32),
            pltpu.SemaphoreType.DMA((3,)),
            pltpu.SemaphoreType.DMA((2, STRIPS)),
            pltpu.SemaphoreType.DMA((steps, 2, STRIPS)),
            pltpu.SemaphoreType.DMA((steps, 2, STRIPS)),
            pltpu.SemaphoreType.DMA((groups,)),
            pltpu.SemaphoreType.DMA((groups,)),
        ],
        compiler_params=pltpu.CompilerParams(
            collective_id=0, has_side_effects=True, vmem_limit_bytes=48 * 1024 * 1024
        ),
        name="steps",
    )(admittance, absorption, source_cell, signal, receivers, pressure, previous, materials)
    return field[steps % 2], field[(steps + 1) % 2], readings


def solution(mesh):
    slab = P(("room", "gx"), None, None)
    return jax.shard_map(
        local,
        mesh=mesh,
        in_specs=(slab, slab, slab, P("room"), P("room"), P("room"), P("room"), P("room")),
        out_specs=(slab, slab, P("room", None)),
        check_vma=False,
    )
```

time: 234 us -> 52.2 us (0.22)
  other arithmetic: 119 us -> 0 us
  Pallas kernels: 0 us -> 39.7 us
  blocking collectives: 33.1 us -> 0 us
  starting transfers between devices: 27.1 us -> 0 us
  local copies, waits for them, and re-layouts: 36.7 us -> 11 us
  between operations: 12.1 us -> 1.3 us
  waiting for transfers between devices: 3.54 us -> 0 us
    div x4 -> x0, other arithmetic: 104 us -> none  [advance(): ((2.0 - courant_sq * inside) * current + courant_sq * summed - (1.0 - los...]
    pallas_call x0 -> x1, Pallas kernels: none -> 39.7 us  [local(): pl.pallas_call(functools.partial(kernel, groups, steps), out_shape=(jax.S...]
    psum x1 -> x0, blocking collectives: 33.1 us -> none  [collect(): return lax.psum(local_values, 'gx')]
    ppermute x8 -> x0, starting transfers between devices: 27.1 us -> none  [the longest x4 21.7 us: extended_2(): lax.ppermute(tail, axis, [(i, (i + 1) % count) for i in range(ends)])]
    concatenate x4 -> x0, other arithmetic: 13.1 us -> none  [extended_2(): jnp.concatenate([lax.ppermute(tail, axis, [(i, (i + 1) % count) for i in...]
    unnamed x32 -> x13, local copies, waits for them, and re-layouts: 15.6 us -> 6.37 us
    slice x7 -> x0, local copies, waits for them, and re-layouts: 8.57 us -> none  [the longest x4 3.23 us: extended_2(): lax.slice_in_dim(cells, cells.shape[dim] - width, cells.shape[dim], axis=...]
    gather x4 -> x0, local copies, waits for them, and re-layouts: 5.82 us -> none  [sample(): return jnp.where(owner_mask, field.reshape(-1)[flat_index], 0.0)]
  transfers between devices with their start and end apart: 8 -> 0, of which waited for: 2 -> 0; matrix products, arithmetic and copies ran while one was open for 9% -> 0% of each run, Pallas kernels for 0% -> 0%
where the time goes in v1:
time: 52.2 us; the launch traced here: 52 us
  Pallas kernels  39.7 us (76%)
  local copies, waits for them, and re-layouts  11 us (21%)
  between operations  1.3 us (2%)
    pallas_call x1, Pallas kernels, local(): pl.pallas_call(functools.partial(kernel, groups, steps), out_shape=(jax.S...  39.7 us
    unnamed x13, local copies, waits for them, and re-layouts  6.37 us
    squeeze x1, local copies, waits for them, and re-layouts, local(): return (field[steps % 2], field[(steps + 1) % 2], readings)  4.63 us

profile of v1, /device:TPU:0, one launch (start us, length us, event | category | flops | bytes accessed | tf_op | source)
XLA Modules:
  0.0 52.0 jit_solution(2175002920522705258)
XLA Ops:
  1.3 0.0 copy-start
  1.3 1.6 %copy-done = f32[8,256,256]{2,1,0:T(8,128)S(1)} copy-done((f32[8,256,256]{2,1,0:T(8,128)S(1)}, f32[8,256,256]{2,1,0:T(8,128)}, u32[]{:S(2)}) %copy-start) | copy-done | bytes 2097176
  2.9 0.0 copy-start.1
  2.9 1.6 %copy-done.1 = f32[8,256,256]{2,1,0:T(8,128)S(1)} copy-done((f32[8,256,256]{2,1,0:T(8,128)S(1)}, f32[8,256,256]{2,1,0:T(8,128)}, u32[]{:S(2)}) %copy-start.1) | copy-done | bytes 2097176
  4.5 0.0 copy-start.2
  4.5 0.7 %copy-done.2 = f32[16]{0:T(128)S(1)} copy-done((f32[16]{0:T(128)S(1)}, f32[16]{0:T(128)}, u32[]{:S(2)}) %copy-start.2) | copy-done | bytes 88
  5.1 0.0 copy-start.3
  5.1 0.7 %copy-done.3 = f32[16]{0:T(128)S(1)} copy-done((f32[16]{0:T(128)S(1)}, f32[16]{0:T(128)}, u32[]{:S(2)}) %copy-start.3) | copy-done | bytes 88
  5.8 0.0 copy-start.4
  5.8 0.7 %copy-done.4 = f32[4]{0:T(128)S(1)} copy-done((f32[4]{0:T(128)S(1)}, f32[4]{0:T(128)}, u32[]{:S(2)}) %copy-start.4) | copy-done | bytes 40
  6.4 0.0 copy-start.5
  6.4 0.7 %copy-done.5 = s32[64]{0:T(128)S(1)} copy-done((s32[64]{0:T(128)S(1)}, s32[64]{0:T(128)}, u32[]{:S(2)}) %copy-start.5) | copy-done | bytes 280
  7.1 39.7 %steps.1 = (f32[2,8,256,256]{3,2,1,0:T(8,128)}, f32[4,64]{1,0:T(4,128)S(1)}) custom-call(f32[16]{0:T(128)S(1)} %copy-done.2, f32[16]{0:T(128)S(1)} %copy-done.3, s32[1]{0:T(128)S(6)} %copy.12.source_ref, f32[4]{0:T(128)S(1)} %copy-done.4, s32[64]{0:T(128)S(1)} %copy-done.5, f32[8,256,256]{2,1,0:T(8,128)S(1)} %copy-done, f32[8,256,256]{2,1,0:T(8,128)S(1)} %copy-done.1, ...), custom_call_target="tpu_custom_call" | custom-call | tf_op jit(solution)/shard_map/steps/pallas_call | solution.py:248
  46.8 4.6 %slice_bitcast_fusion = (f32[8,256,256]{2,1,0:T(8,128)}, f32[8,256,256]{2,1,0:T(8,128)}) fusion(f32[2,8,256,256]{3,2,1,0:T(8,128)} %get-tuple-element.5), kind=kLoop, calls=%fused_computation | loop fusion | bytes 8388608 | tf_op jit(solution)/shard_map/squeeze | solution.py:274
  51.4 0.6 %copy.13 = f32[4,64]{1,0:T(4,128)} copy(f32[4,64]{1,0:T(4,128)S(1)} %get-tuple-element.14) | data formatting | bytes 2048
Async XLA Ops:
  1.3 1.6 %copy-start = (f32[8,256,256]{2,1,0:T(8,128)S(1)}, f32[8,256,256]{2,1,0:T(8,128)}, u32[]{:S(2)}) copy-start(f32[8,256,256]{2,1,0:T(8,128)} %pressure_ref.1) | copy-start | bytes 6291460
  2.9 1.6 %copy-start.1 = (f32[8,256,256]{2,1,0:T(8,128)S(1)}, f32[8,256,256]{2,1,0:T(8,128)}, u32[]{:S(2)}) copy-start(f32[8,256,256]{2,1,0:T(8,128)} %previous_ref.1) | copy-start | bytes 6291460
  4.5 0.7 %copy-start.2 = (f32[16]{0:T(128)S(1)}, f32[16]{0:T(128)}, u32[]{:S(2)}) copy-start(f32[16]{0:T(128)} %adm_ref.1) | copy-start | bytes 196
  5.1 0.7 %copy-start.3 = (f32[16]{0:T(128)S(1)}, f32[16]{0:T(128)}, u32[]{:S(2)}) copy-start(f32[16]{0:T(128)} %abs_ref.1) | copy-start | bytes 196
  5.8 0.7 %copy-start.4 = (f32[4]{0:T(128)S(1)}, f32[4]{0:T(128)}, u32[]{:S(2)}) copy-start(f32[4]{0:T(128)} %signal_ref.1) | copy-start | bytes 52
  6.4 0.7 %copy-start.5 = (s32[64]{0:T(128)S(1)}, s32[64]{0:T(128)}, u32[]{:S(2)}) copy-start(s32[64]{0:T(128)} %recv_ref.1) | copy-start | bytes 772

commit v2 on v1

v2 whole, which is shorter than its diff:
```python
import functools

import jax
import jax.numpy as jnp
from jax import lax
from jax.experimental import pallas as pl
from jax.experimental.pallas import tpu as pltpu
from jax.sharding import PartitionSpec as P

courant = 0.5773502691896258
courant_sq = 1.0 / 3.0

STRIPS = 4
AHEAD = 2


def kernel(
    groups,
    steps,
    adm_hbm,
    abs_hbm,
    source_hbm,
    signal_hbm,
    recv_hbm,
    pressure_ref,
    previous_ref,
    materials_ref,
    field,
    readings_ref,
    adm_ref,
    abs_ref,
    source_ref,
    signal_ref,
    recv_ref,
    small_sem,
    mats,
    coef,
    halo,
    mine,
    gathered,
    load_sem,
    send_sem,
    halo_sem,
    gather_send,
    gather_recv,
):
    layers, size_y, size_z = pressure_ref.shape
    rows = size_y // STRIPS
    receivers = recv_ref.shape[0]
    classes = adm_ref.shape[0]
    me = lax.axis_index("gx")
    start_x = me * layers
    has_left = me > 0
    has_right = me < groups - 1

    def load(which, strip):
        source, target = ((pressure_ref, field.at[0]), (previous_ref, field.at[1]), (materials_ref, mats))[which]
        here = pl.ds(pl.multiple_of(strip * rows, rows), rows)
        return pltpu.make_async_copy(source.at[:, here, :], target.at[:, here, :], load_sem.at[which, strip])

    smalls = [
        pltpu.make_async_copy(source, target, small_sem.at[i])
        for i, (source, target) in enumerate(
            [
                (adm_hbm, adm_ref),
                (abs_hbm, abs_ref),
                (source_hbm, source_ref),
                (signal_hbm, signal_ref),
                (recv_hbm, recv_ref),
            ]
        )
    ]
    for small in smalls:
        small.start()
    for strip in range(STRIPS):
        for which in range(3):
            load(which, strip).start()

    barrier = pltpu.get_barrier_semaphore()

    def greet(hop, carry):
        pl.semaphore_signal(barrier, inc=1, device_id={"gx": lax.rem(me + hop, groups)}, device_id_type=pl.DeviceIdType.MESH)
        return carry

    lax.fori_loop(1, groups, greet, 0)
    pl.semaphore_wait(barrier, groups - 1)

    def send(step, side, strip, source):
        layer = layers - 1 if side == 0 else 0
        return pltpu.make_async_remote_copy(
            src_ref=source.at[layer, pl.ds(pl.multiple_of(strip * rows, rows), rows), :],
            dst_ref=halo.at[step, side, strip],
            send_sem=send_sem.at[step, side, strip],
            recv_sem=halo_sem.at[step, side, strip],
            device_id={"gx": me + 1 if side == 0 else me - 1},
            device_id_type=pl.DeviceIdType.MESH,
        )

    def on_sides(action):
        pl.when(has_right)(lambda: action(0))
        pl.when(has_left)(lambda: action(1))

    for strip in range(AHEAD):
        on_sides(lambda side: send(0, side, strip, pressure_ref).start())

    for small in smalls:
        small.wait()

    lane = lax.broadcasted_iota(jnp.int32, (8, 128), 1)
    outside_lane = lane // classes
    class_lane = lane - outside_lane * classes
    adm_lane = jnp.zeros((8, 128), jnp.float32)
    abs_lane = jnp.zeros((8, 128), jnp.float32)
    for m in range(classes):
        adm_lane = jnp.where(class_lane == m, adm_ref[m], adm_lane)
        abs_lane = jnp.where(class_lane == m, abs_ref[m], abs_lane)
    table = courant_sq / (1.0 + (0.5 * courant * outside_lane.astype(jnp.float32) * adm_lane + abs_lane))

    table_block = jnp.broadcast_to(table[0:1], (rows, 128))

    def fill(layer, row0):
        at_x = start_x + layer
        edge_x = jnp.where((at_x == 0) | (at_x == groups * layers - 1), classes, 0)
        row = row0 + lax.broadcasted_iota(jnp.int32, (rows, 128), 0)
        edge_xy = edge_x + jnp.where((row == 0) | (row == size_y - 1), classes, 0)
        for part in range(size_z // 128):
            cols = pl.ds(part * 128, 128)
            index = mats[layer, pl.ds(row0, rows), cols] + edge_xy
            col = part * 128 + lax.broadcasted_iota(jnp.int32, (rows, 128), 1)
            if part == 0 or part == size_z // 128 - 1:
                index = index + jnp.where((col == 0) | (col == size_z - 1), classes, 0)
            coef[layer, pl.ds(row0, rows), cols] = jnp.take_along_axis(table_block, index, axis=1, mode="promise_in_bounds")

    source = source_ref[0]
    source_x = source // (size_y * size_z) - start_x
    source_y = (source // size_z) % size_y
    source_z = source % size_z

    row_id = lax.broadcasted_iota(jnp.int32, (rows, 128), 0)
    col_id = lax.broadcasted_iota(jnp.int32, (rows, 128), 1)
    parts = size_z // 128
    mine[...] = jnp.zeros(mine.shape, jnp.float32)
    wide = mine.shape[1]
    mine_row = lax.broadcasted_iota(jnp.int32, mine.shape, 0)
    mine_col = lax.broadcasted_iota(jnp.int32, mine.shape, 1)
    lane_row = lax.broadcasted_iota(jnp.int32, (1, size_z), 1)

    def one_layer(step, now, then, strip, layer, low, high):
        row0 = pl.multiple_of(strip * rows, rows)
        here = pl.ds(row0, rows)
        push_x = jnp.where(source_x == layer, signal_ref[step], 0.0)
        above_row = field[now, layer, pl.ds(jnp.maximum(row0 - 1, 0), 1), :]
        below_row = field[now, layer, pl.ds(jnp.minimum(row0 + rows, size_y - 1), 1), :]
        cells = [field[now, layer, here, pl.ds(128 * part, 128)] for part in range(parts)]
        rights = [pltpu.roll(c, 1, 1) for c in cells]
        lefts = [pltpu.roll(c, 127, 1) for c in cells]
        for part in range(parts):
            cols = pl.ds(128 * part, 128)
            c = cells[part]
            above = above_row[:, 128 * part : 128 * part + 128]
            below = below_row[:, 128 * part : 128 * part + 128]
            down = pltpu.roll(c, 1, 0)
            down = jnp.concatenate([jnp.where(row_id[:8] == 0, above, down[:8]), down[8:]], axis=0)
            up = pltpu.roll(c, rows - 1, 0)
            up = jnp.concatenate([up[:-8], jnp.where(row_id[:8] == 7, below, up[-8:])], axis=0)
            total = low(part) + high(part)
            total = total + (down + up)
            total = total + jnp.where(col_id == 0, rights[part - 1] if part else c, rights[part])
            total = total + jnp.where(col_id == 127, lefts[part + 1] if part < parts - 1 else c, lefts[part])
            old = field[then, layer, here, cols]
            following = old + coef[layer, here, cols] * (total - 6.0 * old)
            push = jnp.where(lane_row[:, 128 * part : 128 * part + 128] == source_z, push_x, 0.0)
            following = following + jnp.where(row_id == source_y - row0, push, 0.0)
            field[then, layer, here, cols] = following

    def strip_body(step, strip):
        now = lax.rem(step, 2)
        then = 1 - now
        row0 = pl.multiple_of(strip * rows, rows)
        here = pl.ds(row0, rows)

        @pl.when(step == 0)
        def _():
            load(1, strip).wait()
            load(2, strip).wait()
            pl.when(strip < STRIPS - 1)(lambda: load(0, strip + 1).wait())
            for layer in range(layers):
                fill(layer, row0)
            pl.when(strip < STRIPS - AHEAD)(lambda: on_sides(lambda side: send(0, side, strip + AHEAD, pressure_ref).start()))

        def arrived(side):
            pltpu.make_async_copy(halo.at[step, side, strip], halo.at[step, side, strip], halo_sem.at[step, side, strip]).wait()

        pl.when(has_left)(lambda: arrived(0))
        pl.when(has_right)(lambda: arrived(1))
        @pl.when(step > 0)
        def _():
            on_sides(lambda side: send(step - 1, side, strip, field.at[then]).wait_send())

        def slab(layer):
            return lambda part: field[now, layer, here, pl.ds(128 * part, 128)]

        def side_low(part):
            cols = pl.ds(128 * part, 128)
            return jnp.where(has_left, halo[step, 0, strip, :, cols], field[now, 0, here, cols])

        def side_high(part):
            cols = pl.ds(128 * part, 128)
            return jnp.where(has_right, halo[step, 1, strip, :, cols], field[now, layers - 1, here, cols])

        for layer in [0, layers - 1] + list(range(1, layers - 1)):
            low = side_low if layer == 0 else slab(layer - 1)
            high = side_high if layer == layers - 1 else slab(layer + 1)
            one_layer(step, now, then, strip, layer, low, high)
            if layer == layers - 1:
                pl.when(step < steps - 1)(lambda: on_sides(lambda side: send(step + 1, side, strip, field.at[then]).start()))

    def step_body(step, carry):
        def inner(strip, c):
            strip_body(step, strip)
            return c

        lax.fori_loop(0, STRIPS, inner, 0)
        then = lax.rem(step + 1, 2)
        total = mine[...]
        for k in range(receivers // groups):
            slot = k * groups + me
            cell = recv_ref[slot]
            at_x = jnp.clip(cell // (size_y * size_z) - start_x, 0, layers - 1)
            at_y = (cell // size_z) % size_y
            at_z = cell % size_z
            line = field[then, at_x, pl.ds(at_y, 1), :]
            value = jnp.sum(jnp.where(lane_row == at_z, line, 0.0), axis=1, keepdims=True)
            total = total + jnp.where((mine_row == step) & (mine_col == slot), value, 0.0)
        mine[...] = total
        return carry

    load(0, 0).wait()
    lax.fori_loop(0, steps, step_body, 0)

    def gather_copy(hop):
        peer = lax.rem(me + hop, groups)
        return pltpu.make_async_remote_copy(
            src_ref=mine,
            dst_ref=gathered.at[hop],
            send_sem=gather_send.at[hop],
            recv_sem=gather_recv.at[hop],
            device_id={"gx": peer},
            device_id_type=pl.DeviceIdType.MESH,
        )

    def gather_start(hop, carry):
        gather_copy(hop).start()
        return carry

    lax.fori_loop(1, groups, gather_start, 0)

    for strip in range(STRIPS):
        on_sides(lambda side: send(steps - 1, side, strip, field.at[(steps - 1) % 2]).wait_send())

    def gather_add(hop, total):
        gather_copy(hop).wait()
        return total + gathered[hop]

    total = lax.fori_loop(1, groups, gather_add, mine[...])
    readings_ref[...] = total[0:steps, 0:receivers]


def write_kernel(field, readings, pressure_out, previous_out, readings_out, sems, small_sem):
    layers = pressure_out.shape[0]
    copies = [pltpu.make_async_copy(readings, readings_out, small_sem)]
    for layer in range(layers):
        for which, out in enumerate((pressure_out, previous_out)):
            copies.append(pltpu.make_async_copy(field.at[which, layer], out.at[layer], sems.at[which, layer]))
    for copy in copies:
        copy.start()
    for copy in copies:
        copy.wait()


def local(pressure, previous, materials, admittance, absorption, source_cell, signal, receivers):
    layers, size_y, size_z = pressure.shape
    groups = lax.axis_size("gx")
    steps = signal.shape[0]
    wide = -(-receivers.shape[0] // 128) * 128
    rows = size_y // STRIPS
    vmem = pl.BlockSpec(memory_space=pltpu.VMEM)
    hbm = pl.BlockSpec(memory_space=pltpu.HBM)
    field, readings = pl.pallas_call(
        functools.partial(kernel, groups, steps),
        out_shape=(
            pltpu.VMEM((2, layers, size_y, size_z), jnp.float32),
            pltpu.VMEM((steps, receivers.shape[0]), jnp.float32),
        ),
        in_specs=[hbm] * 8,
        out_specs=(vmem, vmem),
        scratch_shapes=[
            pltpu.SMEM(admittance.shape, jnp.float32),
            pltpu.SMEM(absorption.shape, jnp.float32),
            pltpu.SMEM(source_cell.shape, jnp.int32),
            pltpu.SMEM(signal.shape, jnp.float32),
            pltpu.SMEM(receivers.shape, jnp.int32),
            pltpu.SemaphoreType.DMA((5,)),
            pltpu.VMEM((layers, size_y, size_z), jnp.int32),
            pltpu.VMEM((layers, size_y, size_z), jnp.float32),
            pltpu.VMEM((steps, 2, STRIPS, rows, size_z), jnp.float32),
            pltpu.VMEM((8, wide), jnp.float32),
            pltpu.VMEM((groups, 8, wide), jnp.float32),
            pltpu.SemaphoreType.DMA((3, STRIPS)),
            pltpu.SemaphoreType.DMA((steps, 2, STRIPS)),
            pltpu.SemaphoreType.DMA((steps, 2, STRIPS)),
            pltpu.SemaphoreType.DMA((groups,)),
            pltpu.SemaphoreType.DMA((groups,)),
        ],
        compiler_params=pltpu.CompilerParams(
            collective_id=0, has_side_effects=True, vmem_limit_bytes=59 * 1024 * 1024
        ),
        name="steps",
    )(admittance, absorption, source_cell, signal, receivers, pressure, previous, materials)
    slab = jax.ShapeDtypeStruct((layers, size_y, size_z), jnp.float32)
    return pl.pallas_call(
        write_kernel,
        out_shape=(slab, slab, jax.ShapeDtypeStruct(readings.shape, jnp.float32)),
        in_specs=[pl.BlockSpec(memory_space=pl.ANY)] * 2,
        out_specs=(hbm, hbm, hbm),
        scratch_shapes=[pltpu.SemaphoreType.DMA((2, layers)), pltpu.SemaphoreType.DMA],
        compiler_params=pltpu.CompilerParams(vmem_limit_bytes=1024 * 1024),
        name="write",
    )(field, readings)


def solution(mesh):
    slab = P(("room", "gx"), None, None)
    return jax.shard_map(
        local,
        mesh=mesh,
        in_specs=(slab, slab, slab, P("room"), P("room"), P("room"), P("room"), P("room")),
        out_specs=(slab, slab, P("room", None)),
        check_vma=False,
    )
```

time: 52.2 us -> 40.8 us (0.78)
  local copies, waits for them, and re-layouts: 11 us -> 0 us
    unnamed x13 -> x0, local copies, waits for them, and re-layouts: 6.37 us -> none
    squeeze x1 -> x0, local copies, waits for them, and re-layouts: 4.63 us -> none  [local(): return (field[steps % 2], field[(steps + 1) % 2], readings)]
    pallas_call x1 -> x2, Pallas kernels: 39.7 us -> 39.4 us  [the longest x1 37.2 us: local(): pl.pallas_call(functools.partial(kernel, groups, steps), out_shape=(pltpu...]
where the time goes in v2:
time: 40.8 us; the launch traced here: 40.6 us
  Pallas kernels  39.4 us (97%)
  between operations  1.29 us (3%)
    pallas_call x1, Pallas kernels, local(): pl.pallas_call(functools.partial(kernel, groups, steps), out_shape=(pltpu...  37.2 us
    pallas_call x1, Pallas kernels, local(): pl.pallas_call(write_kernel, out_shape=(slab, slab, jax.ShapeDtypeStruct(...  2.15 us

profile of v2, /device:TPU:0, one launch (start us, length us, event | category | flops | bytes accessed | tf_op | source)
XLA Modules:
  0.0 40.6 jit_solution(2479260986427361803)
XLA Ops:
  1.3 37.2 %steps.1 = (f32[2,8,256,256]{3,2,1,0:T(8,128)S(1)}, f32[4,64]{1,0:T(4,128)S(1)}) custom-call(f32[16]{0:T(128)} %adm_hbm.1, f32[16]{0:T(128)} %abs_hbm.1, s32[1]{0:T(128)S(6)} %copy.11.source_hbm, f32[4]{0:T(128)} %signal_hbm.1, s32[64]{0:T(128)} %recv_hbm.1, f32[8,256,256]{2,1,0:T(8,128)} %pressure_ref.1, f32[8,256,256]{2,1,0:T(8,128)} %previous_ref.1, ...), custom_call_target="tpu_custom_call" | custom-call | tf_op jit(solution)/shard_map/steps/pallas_call | solution.py:289
  38.5 2.1 %write.1 = (f32[8,256,256]{2,1,0:T(8,128)}, f32[8,256,256]{2,1,0:T(8,128)}, f32[4,64]{1,0:T(4,128)}) custom-call(f32[2,8,256,256]{3,2,1,0:T(8,128)S(1)} %get-tuple-element.5.field, f32[4,64]{1,0:T(4,128)S(1)} %get-tuple-element.6.readings), custom_call_target="tpu_custom_call" | custom-call | tf_op jit(solution)/shard_map/write/pallas_call | solution.py:321

commit v3 on v2

--- a/solution.py
+++ b/solution.py
@@ -10,7 +10,7 @@
 courant = 0.5773502691896258
 courant_sq = 1.0 / 3.0
 
-STRIPS = 4
+STRIPS = 2
 AHEAD = 2
 
 
@@ -53,6 +53,13 @@
     has_left = me > 0
     has_right = me < groups - 1
 
+    barrier = pltpu.get_barrier_semaphore()
+
+    def greet(hop, carry):
+        pl.semaphore_signal(barrier, inc=1, device_id={"gx": lax.rem(me + hop, groups)}, device_id_type=pl.DeviceIdType.MESH)
+        return carry
+
+    lax.fori_loop(1, groups, greet, 0, unroll=groups <= 16)
     def load(which, strip):
         source, target = ((pressure_ref, field.at[0]), (previous_ref, field.at[1]), (materials_ref, mats))[which]
         here = pl.ds(pl.multiple_of(strip * rows, rows), rows)
@@ -76,13 +83,6 @@
         for which in range(3):
             load(which, strip).start()
 
-    barrier = pltpu.get_barrier_semaphore()
-
-    def greet(hop, carry):
-        pl.semaphore_signal(barrier, inc=1, device_id={"gx": lax.rem(me + hop, groups)}, device_id_type=pl.DeviceIdType.MESH)
-        return carry
-
-    lax.fori_loop(1, groups, greet, 0)
     pl.semaphore_wait(barrier, groups - 1)
 
     def send(step, side, strip, source):
@@ -131,7 +131,7 @@
                 index = index + jnp.where((col == 0) | (col == size_z - 1), classes, 0)
             coef[layer, pl.ds(row0, rows), cols] = jnp.take_along_axis(table_block, index, axis=1, mode="promise_in_bounds")
 
-    source = source_ref[0]
+    source = source_ref[0, 0]
     source_x = source // (size_y * size_z) - start_x
     source_y = (source // size_z) % size_y
     source_z = source % size_z
@@ -191,11 +191,12 @@
         def arrived(side):
             pltpu.make_async_copy(halo.at[step, side, strip], halo.at[step, side, strip], halo_sem.at[step, side, strip]).wait()
 
-        pl.when(has_left)(lambda: arrived(0))
-        pl.when(has_right)(lambda: arrived(1))
-        @pl.when(step > 0)
-        def _():
-            on_sides(lambda side: send(step - 1, side, strip, field.at[then]).wait_send())
+        def receive():
+            pl.when(has_left)(lambda: arrived(0))
+            pl.when(has_right)(lambda: arrived(1))
+            @pl.when(step > 0)
+            def _():
+                on_sides(lambda side: send(step - 1, side, strip, field.at[then]).wait_send())
 
         def slab(layer):
             return lambda part: field[now, layer, here, pl.ds(128 * part, 128)]
@@ -208,7 +209,9 @@
             cols = pl.ds(128 * part, 128)
             return jnp.where(has_right, halo[step, 1, strip, :, cols], field[now, layers - 1, here, cols])
 
-        for layer in [0, layers - 1] + list(range(1, layers - 1)):
+        for layer in list(range(1, layers - 1)) + [0, layers - 1]:
+            if layer == 0:
+                receive()
             low = side_low if layer == 0 else slab(layer - 1)
             high = side_high if layer == layers - 1 else slab(layer + 1)
             one_layer(step, now, then, strip, layer, low, high)
@@ -253,16 +256,17 @@
         gather_copy(hop).start()
         return carry
 
-    lax.fori_loop(1, groups, gather_start, 0)
+    lax.fori_loop(1, groups, gather_start, 0, unroll=groups <= 16)
 
     for strip in range(STRIPS):
         on_sides(lambda side: send(steps - 1, side, strip, field.at[(steps - 1) % 2]).wait_send())
 
-    def gather_add(hop, total):
+    def gather_wait(hop, carry):
         gather_copy(hop).wait()
-        return total + gathered[hop]
-
-    total = lax.fori_loop(1, groups, gather_add, mine[...])
+        return carry
+
+    lax.fori_loop(1, groups, gather_wait, 0, unroll=groups <= 16)
+    total = lax.fori_loop(1, groups, lambda hop, total: total + gathered[hop], mine[...], unroll=groups <= 16)
     readings_ref[...] = total[0:steps, 0:receivers]
 
 
@@ -297,7 +301,7 @@
         scratch_shapes=[
             pltpu.SMEM(admittance.shape, jnp.float32),
             pltpu.SMEM(absorption.shape, jnp.float32),
-            pltpu.SMEM(source_cell.shape, jnp.int32),
+            pltpu.SMEM((1, 1), jnp.int32),
             pltpu.SMEM(signal.shape, jnp.float32),
             pltpu.SMEM(receivers.shape, jnp.int32),
             pltpu.SemaphoreType.DMA((5,)),
@@ -316,7 +320,7 @@
             collective_id=0, has_side_effects=True, vmem_limit_bytes=59 * 1024 * 1024
         ),
         name="steps",
-    )(admittance, absorption, source_cell, signal, receivers, pressure, previous, materials)
+    )(admittance, absorption, source_cell.reshape(1, 1), signal, receivers, pressure, previous, materials)
     slab = jax.ShapeDtypeStruct((layers, size_y, size_z), jnp.float32)
     return pl.pallas_call(
         write_kernel,

time: 40.8 us -> 38.8 us (0.951)
  Pallas kernels: 39.4 us -> 37.4 us
    pallas_call x1, Pallas kernels: 37.2 us -> 35.2 us  [local(): pl.pallas_call(functools.partial(kernel, groups, steps), out_shape=(pltpu...]
where the time goes in v3:
time: 38.8 us; the launch traced here: 38.7 us
  Pallas kernels  37.4 us (96%)
  between operations  1.29 us (3%)
    pallas_call x1, Pallas kernels, local(): pl.pallas_call(functools.partial(kernel, groups, steps), out_shape=(pltpu...  35.2 us
    pallas_call x1, Pallas kernels, local(): pl.pallas_call(write_kernel, out_shape=(slab, slab, jax.ShapeDtypeStruct(...  2.15 us

profile of v3, /device:TPU:0, one launch (start us, length us, event | category | flops | bytes accessed | tf_op | source)
XLA Modules:
  0.0 38.7 jit_solution(14939106188122397812)
XLA Ops:
  1.3 35.2 %steps.1 = (f32[2,8,256,256]{3,2,1,0:T(8,128)S(1)}, f32[4,64]{1,0:T(4,128)S(1)}) custom-call(f32[16]{0:T(128)} %adm_hbm.1, f32[16]{0:T(128)} %abs_hbm.1, s32[1,1]{1,0:T(1,128)} %bitcast.1.source_hbm, f32[4]{0:T(128)} %signal_hbm.1, s32[64]{0:T(128)} %recv_hbm.1, f32[8,256,256]{2,1,0:T(8,128)} %pressure_ref.1, f32[8,256,256]{2,1,0:T(8,128)} %previous_ref.1, ...), custom_call_target="tpu_custom_call" | custom-call | tf_op jit(solution)/shard_map/steps/pallas_call | solution.py:293
  36.5 2.1 %write.1 = (f32[8,256,256]{2,1,0:T(8,128)}, f32[8,256,256]{2,1,0:T(8,128)}, f32[4,64]{1,0:T(4,128)}) custom-call(f32[2,8,256,256]{3,2,1,0:T(8,128)S(1)} %get-tuple-element.5.field, f32[4,64]{1,0:T(4,128)S(1)} %get-tuple-element.6.readings), custom_call_target="tpu_custom_call" | custom-call | tf_op jit(solution)/shard_map/write/pallas_call | solution.py:325
